TPU v7x, 32 devices: a whole 2x2x4 slice. The times are simulated.
32 devices in a mesh: rec: 4 (over y, x), ctx: 8 (over z, core).
Axes of the slice: x: 2, y: 2, z: 4, core: 2. Of those that a mesh axis runs over, the one named last changes fastest.
Arguments:
- queries: bfloat16 [4, 256, 2048], P('rec', 'ctx'), may hold values from -360 to 360
- grad_out: bfloat16 [4, 256, 2048], P('rec', 'ctx'), may hold values from -6 to 6
- keys: bfloat16 [1024, 2048], P('ctx'), may hold values from -13 to 13
- values: bfloat16 [1024, 2048], P('ctx'), may hold values from -6 to 6
- surv_index: int32 [4, 256], P('rec'), may hold values from 0 to 127, as said below
- counts: int32 [4, 8], P('rec'), may hold values from 1 to 32, as said below
Outputs:
- query_grad: bfloat16 [4, 256, 2048], P('rec', 'ctx')
- key_grad: bfloat16 [1024, 2048], P('ctx', 'rec')
- value_grad: bfloat16 [1024, 2048], P('ctx', 'rec')
Inputs may be any that keep to these rules, and one draw needn't show every extreme that they name: `surv_index`: in each depth and index of ctx the live slots come first and hold distinct positions in increasing order; the other slots hold 0. In each depth and index of ctx whose 32 slots are all live, one live slot holds position 127. `counts`: in every depth some index of ctx has all 32 slots live.
All inputs are finite; a program needn't handle non-finite values.
Results may differ from a plain program's by a relative error of at most 0.0051.
Values may be sent and summed in bfloat16 or wider, within the bound.
A program may use at most 64 MiB of HBM per device.

v0:
```python
import math

import jax
import jax.numpy as jnp
from jax import lax
from jax.sharding import PartitionSpec as P

HEADS = 16
HEAD_DIM = 128


NEG_FILL = -1e30


def joined(shard, axis, combine):
    everything = jax.tree.map(lambda part: lax.all_gather(part, axis), shard)
    leading = jax.tree.map(lambda part: part[0], everything)

    def lap(k, so_far):
        return combine(so_far, jax.tree.map(lambda part: part[k], everything))

    return lax.fori_loop(1, lax.axis_size(axis), lap, leading)


def merge_pair_stats(first_stats, second_stats):
    joint_max = jnp.maximum(first_stats[0], second_stats[0])
    left_scale = jnp.exp(first_stats[0] - joint_max)
    right_scale = jnp.exp(second_stats[0] - joint_max)
    return (joint_max, first_stats[1] * left_scale + second_stats[1] * right_scale)


def body(queries, grad_out, keys, values, surv_index, counts):
    ctx_count = lax.axis_size("ctx")
    my_index = lax.axis_index("ctx")
    cap_here = queries.shape[1]
    feature_cols = queries.shape[2]
    tok_here = keys.shape[0]
    all_slots = cap_here * ctx_count
    block_rows = min(512, all_slots)
    block_count = all_slots // block_rows
    factor = 1.0 / math.sqrt(HEAD_DIM)
    gathered_q, gathered_g = (
        lax.all_gather(queries[0], "ctx", axis=0, tiled=True),
        lax.all_gather(grad_out[0], "ctx", axis=0, tiled=True),
    )
    slot_ids = jnp.arange(all_slots)
    is_live = slot_ids % cap_here < jnp.repeat(counts[0], cap_here)
    query_pos = slot_ids // cap_here * tok_here + surv_index[0]
    gathered_g = jnp.where(is_live[:, None], gathered_g, jnp.zeros_like(gathered_g))
    key_pos = my_index * tok_here + jnp.arange(tok_here)
    keys_split = keys.reshape(tok_here, HEADS, HEAD_DIM)
    value_pieces = values.reshape(tok_here, HEADS, HEAD_DIM)
    query_blocks = gathered_q.reshape(block_count, block_rows, HEADS, HEAD_DIM)
    gradient_tiles = gathered_g.reshape(block_count, block_rows, HEADS, HEAD_DIM)
    pos_blocks = query_pos.reshape(block_count, block_rows)

    def block_scores(query_block, pos_block):
        score_matrix = factor * jnp.einsum(
            "rhd,khd->hrk", query_block, keys_split, preferred_element_type=jnp.float32
        )
        visible = key_pos[None, None, :] <= pos_block[None, :, None]
        return (score_matrix, visible)

    def weight_grads(grad_block):
        return jnp.einsum(
            "rhd,khd->hrk", grad_block, value_pieces, preferred_element_type=jnp.float32
        )

    def as_rows(stacked):
        return stacked.transpose(1, 0, 2).reshape(HEADS, all_slots)

    def as_blocks(per_row):
        return per_row.reshape(HEADS, block_count, block_rows).transpose(1, 0, 2)

    def local_stats(operands):
        query_block, pos_block = operands
        score_matrix, visible = block_scores(query_block, pos_block)
        row_max = jnp.max(jnp.where(visible, score_matrix, NEG_FILL), axis=2)
        row_sum = jnp.sum(
            jnp.where(visible, jnp.exp(score_matrix - row_max[:, :, None]), 0.0), axis=2
        )
        return (row_max, row_sum)

    part_max, part_sum = lax.map(local_stats, (query_blocks, pos_blocks))
    row_max, row_sum = joined((as_rows(part_max), as_rows(part_sum)), "ctx", merge_pair_stats)
    log_total = row_max + jnp.log(row_sum)
    log_blocks = as_blocks(log_total)

    def local_delta(operands):
        query_block, grad_block, pos_block, log_block = operands
        score_matrix, visible = block_scores(query_block, pos_block)
        weights = jnp.where(visible, jnp.exp(score_matrix - log_block[:, :, None]), 0.0)
        return jnp.sum(weights * weight_grads(grad_block), axis=2)

    part_delta = lax.map(local_delta, (query_blocks, gradient_tiles, pos_blocks, log_blocks))
    row_delta = lax.psum(as_rows(part_delta), "ctx")
    log_blocks = as_blocks(log_total)
    delta_blocks = as_blocks(row_delta)

    def block_grads(query_block, grad_block, pos_block, log_block, delta_block):
        score_matrix, visible = block_scores(query_block, pos_block)
        weights = jnp.where(visible, jnp.exp(score_matrix - log_block[:, :, None]), 0.0)
        grad_weights = weight_grads(grad_block)
        grad_scores = (weights * (grad_weights - delta_block[:, :, None])).astype(jnp.bfloat16)
        return (weights, grad_scores)

    def query_product(grad_scores):
        return factor * jnp.einsum(
            "hrk,khd->rhd", grad_scores, keys_split, preferred_element_type=jnp.float32
        )

    def final_block(totals, operands):
        query_block, grad_block, pos_block, log_block, delta_block = operands
        weights, grad_scores = block_grads(
            query_block, grad_block, pos_block, log_block, delta_block
        )
        low_weights = weights.astype(jnp.bfloat16)
        key_part = totals[0] + factor * jnp.einsum(
            "hrk,rhd->khd", grad_scores, query_block, preferred_element_type=jnp.float32
        )
        value_part = totals[1] + jnp.einsum(
            "hrk,rhd->khd", low_weights, grad_block, preferred_element_type=jnp.float32
        )
        return ((key_part, value_part), grad_scores)

    empty_sum = jnp.zeros((tok_here, HEADS, HEAD_DIM), jnp.float32)

    def final_with_query(totals, operands):
        new_totals, grad_scores = final_block(totals, operands)
        return (new_totals, query_product(grad_scores))

    sums, query_terms = lax.scan(
        final_with_query,
        (empty_sum, empty_sum),
        (query_blocks, gradient_tiles, pos_blocks, log_blocks, delta_blocks),
    )
    query_terms = query_terms.reshape(all_slots, feature_cols)
    own_rows = lax.psum_scatter(query_terms, "ctx", scatter_dimension=0, tiled=True)
    key_cols, value_cols = (
        lax.psum_scatter(
            sums[0].reshape(tok_here, feature_cols), "rec", scatter_dimension=1, tiled=True
        ),
        lax.psum_scatter(
            sums[1].reshape(tok_here, feature_cols), "rec", scatter_dimension=1, tiled=True
        ),
    )
    return (
        own_rows.astype(jnp.bfloat16)[None],
        key_cols.astype(jnp.bfloat16),
        value_cols.astype(jnp.bfloat16),
    )


def solution(mesh):
    in_specs = (
        P("rec", "ctx", None),
        P("rec", "ctx", None),
        P("ctx", None),
        P("ctx", None),
        P("rec", None),
        P("rec", None),
    )
    out_specs = (P("rec", "ctx", None), P("ctx", "rec"), P("ctx", "rec"))
    return jax.shard_map(body, mesh=mesh, in_specs=in_specs, out_specs=out_specs, check_vma=False)
```

profile of v0, /device:TPU:0, one launch (start us, length us, event | category | flops | bytes accessed | tf_op | source)
XLA Modules:
  0.0 203.5 jit_solution(6879978723824731101)
XLA Ops:
  7.2 0.0 copy-start
  7.2 0.0 all-gather.9.cloned.1.call-start
  7.2 0.7 all-gather.9.cloned.1.call-update
  7.9 0.0 all-gather.7.cloned.1.call-start
  8.0 0.7 all-gather.7.cloned.1.call-update
  8.7 0.0 reduce-scatter.8.cloned.1.call-start
  8.7 0.7 broadcast_in_dim.98
  9.4 0.1 reshape.93
  9.5 1.3 copy.51
  10.9 0.7 fusion.16
  11.6 0.1 broadcast_compare_fusion
  11.6 22.8 %all-gather.9.cloned.1.call-done = bf16[1,256,2048]{2,1,0:T(8,128)(2,1)} async-done(((bf16[1,32,2048]{2,1,0:T(8,128)(2,1)}), bf16[1,256,2048]{2,1,0:T(8,128)(2,1)}) %all-gather.9.cloned.1.call-update) | async-done | bytes 1048592 | tf_op jit(solution)/shard_map/all_gather | solution.py:44
  34.4 1.4 bitcast_select_fusion
  35.8 1.3 copy.52
  37.1 20.7 %all-gather.7.cloned.1.call-done = bf16[1,256,2048]{2,1,0:T(8,128)(2,1)} async-done(((bf16[1,32,2048]{2,1,0:T(8,128)(2,1)}), bf16[1,256,2048]{2,1,0:T(8,128)(2,1)}) %all-gather.7.cloned.1.call-update) | async-done | bytes 1048592 | tf_op jit(solution)/shard_map/all_gather | solution.py:43
  57.8 2.3 %copy.34 = bf16[1,256,2048]{1,2,0:T(8,128)(2,1)} copy(bf16[1,256,2048]{2,1,0:T(8,128)(2,1)} %all-gather.7.cloned.1.call-done) | data formatting | bytes 2097152 | tf_op jit(solution)/shard_map/all_gather | solution.py:43
  60.1 1.8 select_reduce_fusion.1
  61.8 14.0 %all-gather.1 = f32[128,256]{1,0:T(8,128)S(1)} all-gather(f32[16,256]{1,0:T(8,128)S(1)} %get-tuple-element.234), channel_id=3, replica_groups=mesh['rec'=4,'ctx'=8] {'ctx'}, dimensions={0}, use_global_device_ids=true | all-gather | bytes 147456 | tf_op jit(solution)/shard_map/all_gather | solution.py:16
  75.8 0.5 select_reduce_fusion
  76.3 14.0 %all-gather.2 = f32[128,256]{1,0:T(8,128)S(1)} all-gather(f32[16,256]{1,0:T(8,128)S(1)} %select_reduce_fusion), channel_id=4, replica_groups=mesh['rec'=4,'ctx'=8] {'ctx'}, dimensions={0}, use_global_device_ids=true | all-gather | bytes 147456 | tf_op jit(solution)/shard_map/all_gather | solution.py:16
  90.2 0.3 while.11
  90.6 2.8 %fusion.3 = f32[16,128,128]{2,1,0:T(8,128)} fusion(bf16[256,16,128]{0,2,1:T(8,128)(2,1)} %bitcast.53, f32[16,256,128]{1,2,0:T(8,128)S(1)} %get-tuple-element.235, f32[16,256]{1,0:T(8,128)S(1)} %log_add_fusion, pred[256,128]{0,1:T(8,128)(4,1)S(1)} %broadcast_compare_fusion), kind=kOutput, calls=%fused_computation.13 | convolution fusion | flops 136314880 | bytes 4243456 | tf_op jit(solution)/shard_map/while/body/eval_jaxpr/hrk,rhd->khd/dot_general | solution.py:121
  93.3 2.5 %copy.46 = f32[128,2048]{1,0:T(8,128)} copy(f32[128,2048]{0,1:T(8,128)} %bitcast.59) | data formatting | bytes 2097152 | tf_op jit(solution)/shard_map/reshape | solution.py:144
  95.9 0.0 reduce-scatter.8.cloned.1.call-update
  95.9 0.0 reduce-scatter.6.cloned.1.call-start
  96.0 0.0 copy-done
  96.0 3.2 %multiply_reduce_fusion = (f32[16,256]{1,0:T(8,128)S(1)}, f32[16,256,128]{1,2,0:T(8,128)}) fusion(f32[16,256,128]{1,2,0:T(8,128)S(1)} %get-tuple-element.235, f32[16,256]{1,0:T(8,128)S(1)} %log_add_fusion, pred[256,128]{0,1:T(8,128)(4,1)S(1)} %broadcast_compare_fusion, bf16[256,16,128]{0,2,1:T(8,128)(2,1)} %bitcast.54, bf16[128,2048]{1,0:T(8,128)(2,1)S(1)} %copy-done), kind=kOutput, calls=%fused_computation.6 | convolution fusion | flops 136835072 | bytes 5832704 | tf_op jit(solution)/shard_map/while/body/eval_jaxpr/rhd,khd->hrk/dot_general | solution.py:65
  99.2 27.7 %psum.7 = f32[16,256]{1,0:T(8,128)S(1)} all-reduce(f32[16,256]{1,0:T(8,128)S(1)} %get-tuple-element.236), channel_id=1, replica_groups=mesh['rec'=4,'ctx'=8] {'ctx'}, use_global_device_ids=true, to_apply=%region_5.6 | all-reduce | flops 4096 | bytes 32768 | tf_op jit(solution)/shard_map/psum | solution.py:96
  126.8 0.0 copy-start.1
  126.8 2.2 %multiply_convert_fusion = bf16[16,256,128]{1,2,0:T(8,128)(2,1)S(1)} fusion(f32[16,256,128]{1,2,0:T(8,128)} %get-tuple-element.237, f32[16,256,128]{1,2,0:T(8,128)S(1)} %get-tuple-element.235, f32[16,256]{1,0:T(8,128)S(1)} %psum.7, f32[16,256]{1,0:T(8,128)S(1)} %log_add_fusion, pred[256,128]{0,1:T(8,128)(4,1)S(1)} %broadcast_compare_fusion), kind=kLoop, calls=%fused_computation.5 | loop fusion | flops 3145728 | bytes 5308416 | tf_op jit(solution)/shard_map/while/body/eval_jaxpr/convert_element_type | solution.py:104
  129.1 0.0 copy-done.1
  129.1 0.0 copy-start.2
  129.1 0.4 convolution_multiply_fusion.1
  129.5 0.5 copy-done.2
  130.1 0.0 copy-start.3
  130.1 1.3 copy.43
  131.4 0.0 reduce-scatter.6.cloned.1.call-update
  131.4 0.0 reduce-scatter.4.cloned.1.call-start
  131.5 0.0 copy-done.3
  131.5 1.7 convolution_multiply_fusion
  133.2 2.9 %copy.41 = f32[256,2048]{1,0:T(8,128)} copy(f32[256,2048]{0,1:T(8,128)} %bitcast.55) | data formatting | bytes 4194304 | tf_op jit(solution)/shard_map/reshape | solution.py:137
  136.2 0.0 reduce-scatter.4.cloned.1.call-update
  136.2 0.0 reduce-scatter.8.cloned.1.call-done
  136.2 1.6 convert_element_type.21
  137.8 19.5 %reduce-scatter.6.cloned.1.call-done = f32[128,512]{1,0:T(8,128)} async-done(((f32[128,2048]{1,0:T(8,128)}), f32[128,512]{1,0:T(8,128)}) %reduce-scatter.6.cloned.1.call-update) | async-done | bytes 262160 | tf_op jit(solution)/shard_map/reduce_scatter | solution.py:140
  157.4 1.6 convert_element_type.19
  159.0 36.4 %reduce-scatter.4.cloned.1.call-done = f32[32,2048]{1,0:T(8,128)} async-done(((f32[256,2048]{1,0:T(8,128)}), f32[32,2048]{1,0:T(8,128)}) %reduce-scatter.4.cloned.1.call-update) | async-done | bytes 262160 | tf_op jit(solution)/shard_map/reduce_scatter | solution.py:138
  195.3 1.6 convert_bitcast_fusion
  (12 shorter events, 0.2 us)
Async XLA Ops:
  7.2 88.8 %copy-start = (bf16[128,2048]{1,0:T(8,128)(2,1)S(1)}, bf16[128,2048]{1,0:T(8,128)(2,1)}, u32[]{:S(2)}) copy-start(bf16[128,2048]{1,0:T(8,128)(2,1)} %param.11) | copy-start | bytes 1572868
  7.2 27.3 %all-gather.9.cloned.1.call-start = ((), (), s32[]{:S(2)}) async-start(), calls=%async_computation.7 | async-start | bytes 1179648 | tf_op jit(solution)/shard_map/all_gather | solution.py:44
  7.9 49.9 %all-gather.7.cloned.1.call-start = ((), (), s32[]{:S(2)}) async-start(), calls=%async_computation.6 | async-start | bytes 1179648 | tf_op jit(solution)/shard_map/all_gather | solution.py:43
  8.7 127.5 %reduce-scatter.8.cloned.1.call-start = ((), (), s32[]{:S(2)}) async-start(), calls=%async_computation.5 | async-start | bytes 1310720 | tf_op jit(solution)/shard_map/reduce_scatter | solution.py:143
  95.9 61.4 %reduce-scatter.6.cloned.1.call-start = ((), (), s32[]{:S(2)}) async-start(), calls=%async_computation.4 | async-start | bytes 1310720 | tf_op jit(solution)/shard_map/reduce_scatter | solution.py:140
  126.8 2.2 %copy-start.1 = (bf16[1,256,2048]{1,2,0:T(8,128)(2,1)S(1)}, bf16[1,256,2048]{1,2,0:T(8,128)(2,1)}, u32[]{:S(2)}) copy-start(bf16[1,256,2048]{1,2,0:T(8,128)(2,1)} %copy.34) | copy-start | bytes 3145732
  129.1 1.0 copy-start.2
  130.1 1.4 copy-start.3
  131.4 63.9 %reduce-scatter.4.cloned.1.call-start = ((), (), s32[]{:S(2)}) async-start(), calls=%async_computation.3 | async-start | bytes 2359296 | tf_op jit(solution)/shard_map/reduce_scatter | solution.py:138
Sparse Core Ops, SparseCore 0:
  9.6 24.7 all-gather.8
  36.0 21.7 all-gather.6
  96.0 27.2 reduce-scatter.7
  131.6 25.7 reduce-scatter.5
  159.5 35.7 reduce-scatter.3
where the time goes:
time: 204 us; the launch traced here: 203 us
  waiting for transfers between devices  101 us (50%)
  blocking collectives  55.6 us (27%)
  between operations  13.9 us (7%)
  local copies, waits for them, and re-layouts  13 us (6%)
  matrix products  9.88 us (5%)
  other arithmetic  9.87 us (5%)
    reduce_scatter x1, waiting for transfers between devices, body(): lax.psum_scatter(query_terms, 'ctx', scatter_dimension=0, tiled=True)  36.4 us
    all_gather x2, blocking collectives, joined(): everything = jax.tree.map(lambda part: lax.all_gather(part, axis), shard)  27.9 us
    psum x1, blocking collectives, body(): row_delta = lax.psum(as_rows(part_delta), 'ctx')  27.7 us
    all_gather x1, waiting for transfers between devices, body(): lax.all_gather(grad_out[0], 'ctx', axis=0, tiled=True)  22.8 us
    all_gather x1, waiting for transfers between devices, body(): lax.all_gather(queries[0], 'ctx', axis=0, tiled=True)  20.7 us
    reduce_scatter x1, waiting for transfers between devices, body(): lax.psum_scatter(sums[0].reshape(tok_here, feature_cols), 'rec', scatter_...  19.5 us
  transfers between devices with their start and end apart: 5, of which 4 were waited for; matrix products, arithmetic and copies ran while one was open for 10% of the time, Pallas kernels for 0%

commit v1 on v0

v1 whole, which is shorter than its diff:
```python
import functools
import math

import jax
import jax.numpy as jnp
from jax import lax
from jax.experimental import pallas as pl
from jax.experimental.pallas import tpu as pltpu
from jax.sharding import PartitionSpec as P

HEADS = 16
HEAD_DIM = 128
NEG_FILL = -1e30
MESH = pl.DeviceIdType.MESH
NT = (((1,), (1,)), ((), ()))
TN = (((0,), (0,)), ((), ()))


def kernel(
    recs, ctxs, q_ref, g_ref, k_ref, v_ref, surv_ref, counts_ref,
    dq_ref, dk_ref, dv_ref,
    pos, qg, kv, acc, peer, dq_buf, dkv_buf,
    pos_send, pos_recv, qg_send, qg_recv, kv_send, kv_recv, fwd_send,
    acc_send, acc_recv, dq_send, dq_recv, dkv_send, dkv_recv,
):
    groups = HEADS // recs
    parts = ctxs // groups
    cap = q_ref.shape[1]
    tok = k_ref.shape[0]
    slots = recs * cap
    r = lax.axis_index("rec")
    c = lax.axis_index("ctx")
    z = c // parts
    part = c % parts
    factor = 1.0 / math.sqrt(HEAD_DIM)

    def head_cols(rec, group):
        return pl.ds(pl.multiple_of((rec * groups + group) * HEAD_DIM, HEAD_DIM), HEAD_DIM)

    others = [(dr, dz) for dz in range(groups) for dr in range(recs) if dr or dz]

    def partner(dr, dz):
        return (lax.rem(r + dr, recs), lax.rem(z + dz, groups))

    def sibling(dp):
        return lax.rem(part + dp, parts)

    barrier = pltpu.get_barrier_semaphore()
    for dr, dz in others:
        pr, pz = partner(dr, dz)
        pl.semaphore_signal(barrier, inc=1, device_id=(pr, pz * parts + part), device_id_type=MESH)
    for dp in range(1, parts):
        pl.semaphore_signal(
            barrier, inc=1, device_id=(r, z * parts + sibling(dp)), device_id_type=MESH
        )

    row = jnp.broadcast_to(surv_ref[...], (8, surv_ref.shape[1]))
    lane = lax.broadcasted_iota(jnp.int32, (1, slots), 1)
    here = lane - r * cap
    for zs in range(groups):
        cs = zs * parts + part
        moved = pltpu.roll(row, lax.rem(r * cap - cs * cap + ctxs * cap, ctxs * cap), 1)
        live = (here >= 0) & (here < cap) & (here < counts_ref[0, cs])
        pos[r, zs : zs + 1, :] = jnp.where(live, moved[0:1, 0:slots] + cs * tok + 1, 0)

    mine = []
    rows_r = pl.ds(pl.multiple_of(r * cap, cap), cap)
    for i, ref in enumerate((q_ref, g_ref)):
        mine.append(pltpu.make_async_copy(
            ref.at[0, :, head_cols(r, z)], qg.at[z, i, rows_r, :], qg_recv.at[z]))
    for i, ref in enumerate((k_ref, v_ref)):
        mine.append(pltpu.make_async_copy(ref.at[:, head_cols(r, z)], kv.at[c, i], kv_recv.at[c]))
    for copy in mine:
        copy.start()

    pl.semaphore_wait(barrier, len(others) + parts - 1)

    sends = []

    def send(src, dst, send_sem, recv_sem, device):
        copy = pltpu.make_async_remote_copy(
            src_ref=src, dst_ref=dst, send_sem=send_sem, recv_sem=recv_sem,
            device_id=device, device_id_type=MESH,
        )
        copy.start()
        sends.append(copy)

    for dz in range(1, groups):
        pz = lax.rem(z + dz, groups)
        for i, ref in enumerate((k_ref, v_ref)):
            send(ref.at[:, head_cols(r, pz)], kv.at[c, i], kv_send.at[dz, i], kv_recv.at[c],
                 (r, pz * parts + part))
    for dr in range(1, recs):
        send(pos.at[r], pos.at[r], pos_send.at[dr], pos_recv.at[r], (lax.rem(r + dr, recs), c))
    for dr, dz in others:
        pr, pz = partner(dr, dz)
        for i, ref in enumerate((q_ref, g_ref)):
            send(ref.at[0, :, head_cols(pr, pz)], qg.at[z, i, rows_r, :],
                 qg_send.at[dz, dr, i], qg_recv.at[z], (pr, pz * parts + part))
    for dp in range(1, parts):
        for i, ref in enumerate((k_ref, v_ref)):
            send(ref.at[:, head_cols(r, z)], kv.at[c, i], fwd_send.at[dp, 0, i], kv_recv.at[c],
                 (r, z * parts + sibling(dp)))

    def arrived(ref, sem):
        pltpu.make_async_copy(ref, ref, sem).wait()

    for dz in range(1, groups):
        cs = lax.rem(z + dz, groups) * parts + part
        arrived(kv.at[cs], kv_recv.at[cs])
        for dp in range(1, parts):
            send(kv.at[cs], kv.at[cs], fwd_send.at[dp, dz, 0], kv_recv.at[cs],
                 (r, z * parts + sibling(dp)))
    arrived(kv.at[c], kv_recv.at[c])
    for dr in range(1, recs):
        rs = lax.rem(r + dr, recs)
        arrived(pos.at[rs], pos_recv.at[rs])
    for dz in range(groups):
        for dp in range(1, parts):
            cs = lax.rem(z + dz, groups) * parts + sibling(dp)
            arrived(kv.at[cs], kv_recv.at[cs])

    place = sum(pos[rs] for rs in range(recs)) - 1

    for zs in reversed(range(groups)):
        blocks = (zs + 1) * parts
        length = blocks * tok
        arrived(qg.at[zs], qg_recv.at[zs])
        q, g = qg[zs, 0], qg[zs, 1]
        keys = kv[0:blocks, 0].reshape(length, HEAD_DIM)
        vals = kv[0:blocks, 1].reshape(length, HEAD_DIM)
        scores = lax.dot_general(keys, q, NT, preferred_element_type=jnp.float32)
        seen = lax.broadcasted_iota(jnp.int32, (length, slots), 0) <= place[zs : zs + 1, :]
        scores = jnp.where(seen, scores * (factor * math.log2(math.e)), NEG_FILL)
        top = jnp.maximum(jnp.max(scores, axis=0, keepdims=True), 0.1 * NEG_FILL)
        raw = jnp.exp2(scores - top)
        total = jnp.sum(raw, axis=0, keepdims=True)
        weights = raw * (1.0 / jnp.maximum(total, 1e-30))
        grads = lax.dot_general(vals, g, NT, preferred_element_type=jnp.float32)
        delta = jnp.sum(weights * grads, axis=0, keepdims=True)
        ds = (weights * (grads - delta)).astype(jnp.bfloat16)
        wb = weights.astype(jnp.bfloat16)
        dq = lax.dot_general(ds, keys, TN, preferred_element_type=jnp.float32)
        dq_buf[zs] = (dq * factor).astype(jnp.bfloat16)
        for rd in range(recs):
            src = dq_buf.at[zs, rd * cap : (rd + 1) * cap, :]
            dst = dq_ref.at[0, :, head_cols(r, z)]
            home = (r == rd) & (z == zs)

            @pl.when(home)
            def _():
                pltpu.make_async_copy(src, dst, dq_recv).start()

            @pl.when(jnp.logical_not(home))
            def _():
                pltpu.make_async_remote_copy(
                    src_ref=src, dst_ref=dst, send_sem=dq_send.at[zs, rd], recv_sem=dq_recv,
                    device_id=(rd, zs * parts + part), device_id_type=MESH,
                ).start()

        dk = lax.dot_general(ds, q, (((1,), (0,)), ((), ())), preferred_element_type=jnp.float32)
        dv = lax.dot_general(wb, g, (((1,), (0,)), ((), ())), preferred_element_type=jnp.float32)
        dk = dk.reshape(blocks, tok, HEAD_DIM)
        dv = dv.reshape(blocks, tok, HEAD_DIM)
        if zs == groups - 1:
            acc[0:blocks, 0] = dk
            acc[0:blocks, 1] = dv
        else:
            acc[0:blocks, 0] += dk
            acc[0:blocks, 1] += dv
        for dp in range(1, parts):
            cd = zs * parts + sibling(dp)
            send(acc.at[cd], peer.at[parts - dp, zs], acc_send.at[dp, zs],
                 acc_recv.at[parts - dp, zs], (r, z * parts + sibling(dp)))

    for zs in reversed(range(groups)):
        dkv = acc[zs * parts + part]
        for dp in range(1, parts):
            arrived(peer.at[dp, zs], acc_recv.at[dp, zs])
            dkv += peer[dp, zs]
        dkv_buf[zs, 0] = (dkv[0] * factor).astype(jnp.bfloat16)
        dkv_buf[zs, 1] = dkv[1].astype(jnp.bfloat16)
        cols = pl.ds(pl.multiple_of(z * HEAD_DIM, HEAD_DIM), HEAD_DIM)
        for i, ref in enumerate((dk_ref, dv_ref)):

            @pl.when(z == zs)
            def _():
                pltpu.make_async_copy(dkv_buf.at[zs, i], ref.at[:, cols], dkv_recv.at[i]).start()

            @pl.when(z != zs)
            def _():
                pltpu.make_async_remote_copy(
                    src_ref=dkv_buf.at[zs, i], dst_ref=ref.at[:, cols],
                    send_sem=dkv_send.at[zs, i], recv_sem=dkv_recv.at[i],
                    device_id=(r, zs * parts + part), device_id_type=MESH,
                ).start()

    for copy in sends:
        copy.wait_send()
    for zs in range(groups):
        for rd in range(recs):

            @pl.when(jnp.logical_not((r == rd) & (z == zs)))
            def _():
                arrived(dq_buf.at[zs, rd * cap : (rd + 1) * cap, :], dq_send.at[zs, rd])

        for i in range(2):

            @pl.when(z != zs)
            def _():
                arrived(dkv_buf.at[zs, i], dkv_send.at[zs, i])

    arrived(dq_ref, dq_recv)
    arrived(dk_ref, dkv_recv.at[0])
    arrived(dv_ref, dkv_recv.at[1])


def body(queries, grad_out, keys, values, surv_index, counts):
    recs = lax.axis_size("rec")
    ctxs = lax.axis_size("ctx")
    cap, tok = queries.shape[1], keys.shape[0]
    groups = HEADS // recs
    parts = ctxs // groups
    slots = recs * cap
    dma = pltpu.SemaphoreType.DMA
    anywhere = pl.BlockSpec(memory_space=pl.ANY)
    return pl.pallas_call(
        functools.partial(kernel, recs, ctxs),
        out_shape=(
            jax.ShapeDtypeStruct(queries.shape, jnp.bfloat16),
            jax.ShapeDtypeStruct((tok, groups * HEAD_DIM), jnp.bfloat16),
            jax.ShapeDtypeStruct((tok, groups * HEAD_DIM), jnp.bfloat16),
        ),
        in_specs=[anywhere] * 4 + [
            pl.BlockSpec(memory_space=pltpu.VMEM),
            pl.BlockSpec(memory_space=pltpu.SMEM),
        ],
        out_specs=(anywhere,) * 3,
        scratch_shapes=[
            pltpu.VMEM((recs, 8, slots), jnp.int32),
            pltpu.VMEM((groups, 2, slots, HEAD_DIM), jnp.bfloat16),
            pltpu.VMEM((ctxs, 2, tok, HEAD_DIM), jnp.bfloat16),
            pltpu.VMEM((ctxs, 2, tok, HEAD_DIM), jnp.float32),
            pltpu.VMEM((parts, groups, 2, tok, HEAD_DIM), jnp.float32),
            pltpu.VMEM((groups, slots, HEAD_DIM), jnp.bfloat16),
            pltpu.VMEM((groups, 2, tok, HEAD_DIM), jnp.bfloat16),
            dma((recs,)), dma((recs,)),
            dma((groups, recs, 2)), dma((groups,)),
            dma((groups, 2)), dma((ctxs,)),
            dma((parts, groups, 2)),
            dma((parts, groups)), dma((parts, groups)),
            dma((groups, recs)), dma,
            dma((groups, 2)), dma((2,)),
        ],
        compiler_params=pltpu.CompilerParams(
            collective_id=0, has_side_effects=True, vmem_limit_bytes=48 * 2**20
        ),
        cost_estimate=pl.CostEstimate(
            flops=10 * groups * slots * ctxs * tok * HEAD_DIM,
            bytes_accessed=4 * ctxs * tok * HEAD_DIM * 2,
            transcendentals=groups * slots * ctxs * tok,
        ),
    )(queries, grad_out, keys, values, surv_index, counts)


def solution(mesh):
    in_specs = (
        P("rec", "ctx", None),
        P("rec", "ctx", None),
        P("ctx", None),
        P("ctx", None),
        P("rec", None),
        P("rec", None),
    )
    out_specs = (P("rec", "ctx", None), P("ctx", "rec"), P("ctx", "rec"))
    return jax.shard_map(body, mesh=mesh, in_specs=in_specs, out_specs=out_specs, check_vma=False)
```

time: 204 us -> 40 us (0.20)
  waiting for transfers between devices: 101 us -> 0 us
  blocking collectives: 55.6 us -> 0 us
  Pallas kernels: 0 us -> 31.9 us
  between operations: 13.9 us -> 0.65 us
  matrix products: 9.88 us -> 0 us
  other arithmetic: 9.87 us -> 0 us
  local copies, waits for them, and re-layouts: 13 us -> 7.18 us
    reduce_scatter x3 -> x0, waiting for transfers between devices: 55.9 us -> none  [the longest x1 36.4 us: body(): lax.psum_scatter(query_terms, 'ctx', scatter_dimension=0, tiled=True)]
    all_gather x2 -> x0, waiting for transfers between devices: 43.5 us -> none  [the longest x1 22.8 us: body(): lax.all_gather(grad_out[0], 'ctx', axis=0, tiled=True)]
    pallas_call x0 -> x1, Pallas kernels: none -> 31.9 us  [body(): pl.pallas_call(functools.partial(kernel, recs, ctxs), out_shape=(jax.Shap...]
    all_gather x2 -> x0, blocking collectives: 27.9 us -> none  [joined(): everything = jax.tree.map(lambda part: lax.all_gather(part, axis), shard)]
    psum x1 -> x0, blocking collectives: 27.7 us -> none  [body(): row_delta = lax.psum(as_rows(part_delta), 'ctx')]
    dot_general x5 -> x0, matrix products: 9.88 us -> none  [the longest x1 3.18 us: weight_grads(): jnp.einsum('rhd,khd->hrk', grad_block, value_pieces, preferred_element_ty...]
    reshape x5 -> x0, local copies, waits for them, and re-layouts: 8.19 us -> none  [the longest x1 2.93 us: body(): query_terms = query_terms.reshape(all_slots, feature_cols)]
    unnamed x8 -> x15, local copies, waits for them, and re-layouts: 0.54 us -> 7.18 us
  transfers between devices with their start and end apart: 5 -> 0, of which waited for: 4 -> 0; matrix products, arithmetic and copies ran while one was open for 10% -> 0% of each run, Pallas kernels for 0% -> 0%
where the time goes in v1:
time: 40 us; the launch traced here: 39.8 us
  Pallas kernels  31.9 us (80%)
  local copies, waits for them, and re-layouts  7.18 us (18%)
  between operations  0.65 us (2%)
    pallas_call x1, Pallas kernels, body(): pl.pallas_call(functools.partial(kernel, recs, ctxs), out_shape=(jax.Shap...  31.9 us
    unnamed x15, local copies, waits for them, and re-layouts  7.18 us

profile of v1, /device:TPU:0, one launch (start us, length us, event | category | flops | bytes accessed | tf_op | source)
XLA Modules:
  0.0 39.8 jit_solution(1739026020516138241)
XLA Ops:
  0.6 0.0 copy-start
  0.6 1.0 %copy-done = bf16[128,2048]{1,0:T(8,128)(2,1)S(1)} copy-done((bf16[128,2048]{1,0:T(8,128)(2,1)S(1)}, bf16[128,2048]{1,0:T(8,128)(2,1)}, u32[]{:S(2)}) %copy-start) | copy-done | bytes 524312
  1.7 0.0 copy-start.1
  1.7 1.0 %copy-done.1 = bf16[128,2048]{1,0:T(8,128)(2,1)S(1)} copy-done((bf16[128,2048]{1,0:T(8,128)(2,1)S(1)}, bf16[128,2048]{1,0:T(8,128)(2,1)}, u32[]{:S(2)}) %copy-start.1) | copy-done | bytes 524312
  2.7 0.0 copy-start.2
  2.7 0.9 %copy-done.2 = bf16[1,32,2048]{2,1,0:T(8,128)(2,1)S(1)} copy-done((bf16[1,32,2048]{2,1,0:T(8,128)(2,1)S(1)}, bf16[1,32,2048]{2,1,0:T(8,128)(2,1)}, u32[]{:S(2)}) %copy-start.2) | copy-done | bytes 131096
  3.6 0.0 copy-start.3
  3.6 0.9 %copy-done.3 = bf16[1,32,2048]{2,1,0:T(8,128)(2,1)S(1)} copy-done((bf16[1,32,2048]{2,1,0:T(8,128)(2,1)S(1)}, bf16[1,32,2048]{2,1,0:T(8,128)(2,1)}, u32[]{:S(2)}) %copy-start.3) | copy-done | bytes 131096
  4.5 0.0 copy-start.4
  4.5 0.7 %copy-done.4 = s32[1,256]{1,0:T(1,128)S(1)} copy-done((s32[1,256]{1,0:T(1,128)S(1)}, s32[1,256]{1,0:T(1,128)}, u32[]{:S(2)}) %copy-start.4) | copy-done | bytes 1048
  5.2 0.0 copy-start.5
  5.2 0.7 %copy-done.5 = s32[1,8]{1,0:T(1,128)S(1)} copy-done((s32[1,8]{1,0:T(1,128)S(1)}, s32[1,8]{1,0:T(1,128)}, u32[]{:S(2)}) %copy-start.5) | copy-done | bytes 56
  5.9 31.9 %shard_map.85 = (bf16[1,32,2048]{2,1,0:T(8,128)(2,1)S(1)}, bf16[128,512]{1,0:T(8,128)(2,1)S(1)}, bf16[128,512]{1,0:T(8,128)(2,1)S(1)}) custom-call(bf16[1,32,2048]{2,1,0:T(8,128)(2,1)S(1)} %copy-done.2, bf16[1,32,2048]{2,1,0:T(8,128)(2,1)S(1)} %copy-done.3, bf16[128,2048]{1,0:T(8,128)(2,1)S(1)} %copy-done, bf16[128,2048]{1,0:T(8,128)(2,1)S(1)} %copy-done.1, ...), custom_call_target="tpu_custom_call" | custom-call | flops 671088640 | bytes 1048576 | tf_op jit(solution)/shard_map/pallas_call | solution.py:227
  37.8 0.7 %copy.12 = bf16[1,32,2048]{2,1,0:T(8,128)(2,1)} copy(bf16[1,32,2048]{2,1,0:T(8,128)(2,1)S(1)} %get-tuple-element.6) | data formatting | bytes 262144
  38.5 0.7 %copy.13 = bf16[128,512]{1,0:T(8,128)(2,1)} copy(bf16[128,512]{1,0:T(8,128)(2,1)S(1)} %get-tuple-element.7) | data formatting | bytes 262144
  39.1 0.7 %copy.14 = bf16[128,512]{1,0:T(8,128)(2,1)} copy(bf16[128,512]{1,0:T(8,128)(2,1)S(1)} %get-tuple-element.8) | data formatting | bytes 262144
Async XLA Ops:
  0.6 1.0 %copy-start = (bf16[128,2048]{1,0:T(8,128)(2,1)S(1)}, bf16[128,2048]{1,0:T(8,128)(2,1)}, u32[]{:S(2)}) copy-start(bf16[128,2048]{1,0:T(8,128)(2,1)} %k_ref.1) | copy-start | bytes 1572868
  1.7 1.0 %copy-start.1 = (bf16[128,2048]{1,0:T(8,128)(2,1)S(1)}, bf16[128,2048]{1,0:T(8,128)(2,1)}, u32[]{:S(2)}) copy-start(bf16[128,2048]{1,0:T(8,128)(2,1)} %v_ref.1) | copy-start | bytes 1572868
  2.7 0.9 %copy-start.2 = (bf16[1,32,2048]{2,1,0:T(8,128)(2,1)S(1)}, bf16[1,32,2048]{2,1,0:T(8,128)(2,1)}, u32[]{:S(2)}) copy-start(bf16[1,32,2048]{2,1,0:T(8,128)(2,1)} %q_ref.1) | copy-start | bytes 393220
  3.6 0.9 %copy-start.3 = (bf16[1,32,2048]{2,1,0:T(8,128)(2,1)S(1)}, bf16[1,32,2048]{2,1,0:T(8,128)(2,1)}, u32[]{:S(2)}) copy-start(bf16[1,32,2048]{2,1,0:T(8,128)(2,1)} %g_ref.1) | copy-start | bytes 393220
  4.5 0.7 %copy-start.4 = (s32[1,256]{1,0:T(1,128)S(1)}, s32[1,256]{1,0:T(1,128)}, u32[]{:S(2)}) copy-start(s32[1,256]{1,0:T(1,128)} %surv_ref.1) | copy-start | bytes 3076
  5.2 0.7 %copy-start.5 = (s32[1,8]{1,0:T(1,128)S(1)}, s32[1,8]{1,0:T(1,128)}, u32[]{:S(2)}) copy-start(s32[1,8]{1,0:T(1,128)} %counts_ref.1) | copy-start | bytes 100

commit v2 on v1

--- a/solution.py
+++ b/solution.py
@@ -19,8 +19,8 @@
 def kernel(
     recs, ctxs, q_ref, g_ref, k_ref, v_ref, surv_ref, counts_ref,
     dq_ref, dk_ref, dv_ref,
-    pos, qg, kv, acc, peer, dq_buf, dkv_buf,
-    pos_send, pos_recv, qg_send, qg_recv, kv_send, kv_recv, fwd_send,
+    surv, live_counts, pos, qg, kv, acc, peer, dq_buf, dkv_buf,
+    int_sem, pos_send, pos_recv, qg_send, qg_recv, kv_send, kv_recv, fwd_send,
     acc_send, acc_recv, dq_send, dq_recv, dkv_send, dkv_recv,
 ):
     groups = HEADS // recs
@@ -45,6 +45,13 @@
     def sibling(dp):
         return lax.rem(part + dp, parts)
 
+    ints = [
+        pltpu.make_async_copy(surv_ref, surv, int_sem.at[0]),
+        pltpu.make_async_copy(counts_ref, live_counts, int_sem.at[1]),
+    ]
+    for copy in ints:
+        copy.start()
+
     barrier = pltpu.get_barrier_semaphore()
     for dr, dz in others:
         pr, pz = partner(dr, dz)
@@ -53,15 +60,6 @@
         pl.semaphore_signal(
             barrier, inc=1, device_id=(r, z * parts + sibling(dp)), device_id_type=MESH
         )
-
-    row = jnp.broadcast_to(surv_ref[...], (8, surv_ref.shape[1]))
-    lane = lax.broadcasted_iota(jnp.int32, (1, slots), 1)
-    here = lane - r * cap
-    for zs in range(groups):
-        cs = zs * parts + part
-        moved = pltpu.roll(row, lax.rem(r * cap - cs * cap + ctxs * cap, ctxs * cap), 1)
-        live = (here >= 0) & (here < cap) & (here < counts_ref[0, cs])
-        pos[r, zs : zs + 1, :] = jnp.where(live, moved[0:1, 0:slots] + cs * tok + 1, 0)
 
     mine = []
     rows_r = pl.ds(pl.multiple_of(r * cap, cap), cap)
@@ -72,6 +70,17 @@
         mine.append(pltpu.make_async_copy(ref.at[:, head_cols(r, z)], kv.at[c, i], kv_recv.at[c]))
     for copy in mine:
         copy.start()
+
+    for copy in ints:
+        copy.wait()
+    row = jnp.broadcast_to(surv[...], (8, surv.shape[1]))
+    lane = lax.broadcasted_iota(jnp.int32, (1, slots), 1)
+    here = lane - r * cap
+    for zs in range(groups):
+        cs = zs * parts + part
+        moved = pltpu.roll(row, lax.rem(r * cap - cs * cap + ctxs * cap, ctxs * cap), 1)
+        live = (here >= 0) & (here < cap) & (here < live_counts[0, cs])
+        pos[r, zs : zs + 1, :] = jnp.where(live, moved[0:1, 0:slots] + cs * tok + 1, 0)
 
     pl.semaphore_wait(barrier, len(others) + parts - 1)
 
@@ -121,6 +130,28 @@
             arrived(kv.at[cs], kv_recv.at[cs])
 
     place = sum(pos[rs] for rs in range(recs)) - 1
+
+    def finish(zs):
+        dkv = acc[zs * parts + part]
+        for dp in range(1, parts):
+            arrived(peer.at[dp, zs], acc_recv.at[dp, zs])
+            dkv += peer[dp, zs]
+        dkv_buf[zs, 0] = (dkv[0] * factor).astype(jnp.bfloat16)
+        dkv_buf[zs, 1] = dkv[1].astype(jnp.bfloat16)
+        cols = pl.ds(pl.multiple_of(z * HEAD_DIM, HEAD_DIM), HEAD_DIM)
+        for i, ref in enumerate((dk_ref, dv_ref)):
+
+            @pl.when(z == zs)
+            def _():
+                pltpu.make_async_copy(dkv_buf.at[zs, i], ref.at[:, cols], dkv_recv.at[i]).start()
+
+            @pl.when(z != zs)
+            def _():
+                pltpu.make_async_remote_copy(
+                    src_ref=dkv_buf.at[zs, i], dst_ref=ref.at[:, cols],
+                    send_sem=dkv_send.at[zs, i], recv_sem=dkv_recv.at[i],
+                    device_id=(r, zs * parts + part), device_id_type=MESH,
+                ).start()
 
     for zs in reversed(range(groups)):
         blocks = (zs + 1) * parts
@@ -172,28 +203,10 @@
             cd = zs * parts + sibling(dp)
             send(acc.at[cd], peer.at[parts - dp, zs], acc_send.at[dp, zs],
                  acc_recv.at[parts - dp, zs], (r, z * parts + sibling(dp)))
-
-    for zs in reversed(range(groups)):
-        dkv = acc[zs * parts + part]
-        for dp in range(1, parts):
-            arrived(peer.at[dp, zs], acc_recv.at[dp, zs])
-            dkv += peer[dp, zs]
-        dkv_buf[zs, 0] = (dkv[0] * factor).astype(jnp.bfloat16)
-        dkv_buf[zs, 1] = dkv[1].astype(jnp.bfloat16)
-        cols = pl.ds(pl.multiple_of(z * HEAD_DIM, HEAD_DIM), HEAD_DIM)
-        for i, ref in enumerate((dk_ref, dv_ref)):
-
-            @pl.when(z == zs)
-            def _():
-                pltpu.make_async_copy(dkv_buf.at[zs, i], ref.at[:, cols], dkv_recv.at[i]).start()
-
-            @pl.when(z != zs)
-            def _():
-                pltpu.make_async_remote_copy(
-                    src_ref=dkv_buf.at[zs, i], dst_ref=ref.at[:, cols],
-                    send_sem=dkv_send.at[zs, i], recv_sem=dkv_recv.at[i],
-                    device_id=(r, zs * parts + part), device_id_type=MESH,
-                ).start()
+        if zs < groups - 1:
+            finish(zs + 1)
+    finish(0)
+
 
     for copy in sends:
         copy.wait_send()
@@ -213,6 +226,17 @@
     arrived(dq_ref, dq_recv)
     arrived(dk_ref, dkv_recv.at[0])
     arrived(dv_ref, dkv_recv.at[1])
+
+
+def hand_over(a, b, c, a_out, b_out, c_out, sem):
+    copies = [
+        pltpu.make_async_copy(src, dst, sem.at[i])
+        for i, (src, dst) in enumerate(((a, a_out), (b, b_out), (c, c_out)))
+    ]
+    for copy in copies:
+        copy.start()
+    for copy in copies:
+        copy.wait()
 
 
 def body(queries, grad_out, keys, values, surv_index, counts):
@@ -223,20 +247,19 @@
     parts = ctxs // groups
     slots = recs * cap
     dma = pltpu.SemaphoreType.DMA
-    anywhere = pl.BlockSpec(memory_space=pl.ANY)
-    return pl.pallas_call(
+    anywhere = pl.BlockSpec(memory_space=pltpu.HBM)
+    results = pl.pallas_call(
         functools.partial(kernel, recs, ctxs),
         out_shape=(
             jax.ShapeDtypeStruct(queries.shape, jnp.bfloat16),
             jax.ShapeDtypeStruct((tok, groups * HEAD_DIM), jnp.bfloat16),
             jax.ShapeDtypeStruct((tok, groups * HEAD_DIM), jnp.bfloat16),
         ),
-        in_specs=[anywhere] * 4 + [
-            pl.BlockSpec(memory_space=pltpu.VMEM),
-            pl.BlockSpec(memory_space=pltpu.SMEM),
-        ],
+        in_specs=[anywhere] * 6,
         out_specs=(anywhere,) * 3,
         scratch_shapes=[
+            pltpu.VMEM(surv_index.shape, jnp.int32),
+            pltpu.SMEM(counts.shape, jnp.int32),
             pltpu.VMEM((recs, 8, slots), jnp.int32),
             pltpu.VMEM((groups, 2, slots, HEAD_DIM), jnp.bfloat16),
             pltpu.VMEM((ctxs, 2, tok, HEAD_DIM), jnp.bfloat16),
@@ -244,7 +267,7 @@
             pltpu.VMEM((parts, groups, 2, tok, HEAD_DIM), jnp.float32),
             pltpu.VMEM((groups, slots, HEAD_DIM), jnp.bfloat16),
             pltpu.VMEM((groups, 2, tok, HEAD_DIM), jnp.bfloat16),
-            dma((recs,)), dma((recs,)),
+            dma((2,)), dma((recs,)), dma((recs,)),
             dma((groups, recs, 2)), dma((groups,)),
             dma((groups, 2)), dma((ctxs,)),
             dma((parts, groups, 2)),
@@ -253,7 +276,7 @@
             dma((groups, 2)), dma((2,)),
         ],
         compiler_params=pltpu.CompilerParams(
-            collective_id=0, has_side_effects=True, vmem_limit_bytes=48 * 2**20
+            collective_id=0, has_side_effects=True, vmem_limit_bytes=64 * 2**20
         ),
         cost_estimate=pl.CostEstimate(
             flops=10 * groups * slots * ctxs * tok * HEAD_DIM,
@@ -261,6 +284,14 @@
             transcendentals=groups * slots * ctxs * tok,
         ),
     )(queries, grad_out, keys, values, surv_index, counts)
+    return pl.pallas_call(
+        hand_over,
+        out_shape=tuple(jax.ShapeDtypeStruct(a.shape, a.dtype) for a in results),
+        in_specs=[anywhere] * 3,
+        out_specs=(anywhere,) * 3,
+        scratch_shapes=[dma((3,))],
+        compiler_params=pltpu.CompilerParams(vmem_limit_bytes=64 * 2**20),
+    )(*results)
 
 
 def solution(mesh):

time: 40 us -> 46.2 us (1.16)
  Pallas kernels: 31.9 us -> 45.3 us
  local copies, waits for them, and re-layouts: 7.18 us -> 0 us
    pallas_call x0 -> x1, Pallas kernels: none -> 13 us  [body(): pl.pallas_call(hand_over, out_shape=tuple((jax.ShapeDtypeStruct(a.shape,...]
    unnamed x15 -> x0, local copies, waits for them, and re-layouts: 7.18 us -> none
where the time goes in v2:
time: 46.2 us; the launch traced here: 46 us
  Pallas kernels  45.3 us (98%)
  between operations  0.64 us (1%)
    pallas_call x1, Pallas kernels, body(): pl.pallas_call(functools.partial(kernel, recs, ctxs), out_shape=(jax.Shap...  32.3 us
    pallas_call x1, Pallas kernels, body(): pl.pallas_call(hand_over, out_shape=tuple((jax.ShapeDtypeStruct(a.shape,...  13 us

profile of v2, /device:TPU:0, one launch (start us, length us, event | category | flops | bytes accessed | tf_op | source)
XLA Modules:
  0.0 46.0 jit_solution(14787848701086155462)
XLA Ops:
  0.6 32.3 %shard_map.85 = (bf16[1,32,2048]{2,1,0:T(8,128)(2,1)}, bf16[128,512]{1,0:T(8,128)(2,1)}, bf16[128,512]{1,0:T(8,128)(2,1)}) custom-call(bf16[1,32,2048]{2,1,0:T(8,128)(2,1)} %q_ref.1, bf16[1,32,2048]{2,1,0:T(8,128)(2,1)} %g_ref.1, bf16[128,2048]{1,0:T(8,128)(2,1)} %k_ref.1, bf16[128,2048]{1,0:T(8,128)(2,1)} %v_ref.1, s32[1,256]{1,0:T(1,128)} %surv_ref.1, ...), custom_call_target="tpu_custom_call" | custom-call | flops 671088640 | bytes 1048576 | tf_op jit(solution)/shard_map/pallas_call | solution.py:251
  32.9 13.0 %shard_map.86 = (bf16[1,32,2048]{2,1,0:T(8,128)(2,1)}, bf16[128,512]{1,0:T(8,128)(2,1)}, bf16[128,512]{1,0:T(8,128)(2,1)}) custom-call(bf16[1,32,2048]{2,1,0:T(8,128)(2,1)} %get-tuple-element.6.a, bf16[128,512]{1,0:T(8,128)(2,1)} %get-tuple-element.7.b, bf16[128,512]{1,0:T(8,128)(2,1)} %get-tuple-element.8.c), custom_call_target="tpu_custom_call" | custom-call | tf_op jit(solution)/shard_map/pallas_call | solution.py:287

commit v3 on v2

--- a/solution.py
+++ b/solution.py
@@ -228,14 +228,16 @@
     arrived(dv_ref, dkv_recv.at[1])
 
 
-def hand_over(a, b, c, a_out, b_out, c_out, sem):
-    copies = [
-        pltpu.make_async_copy(src, dst, sem.at[i])
-        for i, (src, dst) in enumerate(((a, a_out), (b, b_out), (c, c_out)))
-    ]
-    for copy in copies:
+def hand_over(a, b, c, a_out, b_out, c_out, a_here, b_here, c_here, sem):
+    trios = ((a, a_here, a_out), (b, b_here, b_out), (c, c_here, c_out))
+    into = [pltpu.make_async_copy(src, mid, sem.at[0, i]) for i, (src, mid, _) in enumerate(trios)]
+    out = [pltpu.make_async_copy(mid, dst, sem.at[1, i]) for i, (_, mid, dst) in enumerate(trios)]
+    for copy in into:
         copy.start()
-    for copy in copies:
+    for arriving, leaving in zip(into, out):
+        arriving.wait()
+        leaving.start()
+    for copy in out:
         copy.wait()
 
 
@@ -289,7 +291,7 @@
         out_shape=tuple(jax.ShapeDtypeStruct(a.shape, a.dtype) for a in results),
         in_specs=[anywhere] * 3,
         out_specs=(anywhere,) * 3,
-        scratch_shapes=[dma((3,))],
+        scratch_shapes=[pltpu.VMEM(a.shape, a.dtype) for a in results] + [dma((2, 3))],
         compiler_params=pltpu.CompilerParams(vmem_limit_bytes=64 * 2**20),
     )(*results)
 

time: 46.2 us -> 34.9 us (0.76)
  Pallas kernels: 45.3 us -> 34 us
    pallas_call x1, Pallas kernels: 13 us -> 1.74 us  [body(): pl.pallas_call(hand_over, out_shape=tuple((jax.ShapeDtypeStruct(a.shape,...]
where the time goes in v3:
time: 34.9 us; the launch traced here: 34.7 us
  Pallas kernels  34 us (97%)
  between operations  0.64 us (2%)
    pallas_call x1, Pallas kernels, body(): pl.pallas_call(functools.partial(kernel, recs, ctxs), out_shape=(jax.Shap...  32.3 us
    pallas_call x1, Pallas kernels, body(): pl.pallas_call(hand_over, out_shape=tuple((jax.ShapeDtypeStruct(a.shape,...  1.74 us

profile of v3, /device:TPU:0, one launch (start us, length us, event | category | flops | bytes accessed | tf_op | source)
XLA Modules:
  0.0 34.7 jit_solution(17663934791373734745)
XLA Ops:
  0.6 32.3 %shard_map.85 = (bf16[1,32,2048]{2,1,0:T(8,128)(2,1)}, bf16[128,512]{1,0:T(8,128)(2,1)}, bf16[128,512]{1,0:T(8,128)(2,1)}) custom-call(bf16[1,32,2048]{2,1,0:T(8,128)(2,1)} %q_ref.1, bf16[1,32,2048]{2,1,0:T(8,128)(2,1)} %g_ref.1, bf16[128,2048]{1,0:T(8,128)(2,1)} %k_ref.1, bf16[128,2048]{1,0:T(8,128)(2,1)} %v_ref.1, s32[1,256]{1,0:T(1,128)} %surv_ref.1, ...), custom_call_target="tpu_custom_call" | custom-call | flops 671088640 | bytes 1048576 | tf_op jit(solution)/shard_map/pallas_call | solution.py:253
  32.9 1.7 %shard_map.86 = (bf16[1,32,2048]{2,1,0:T(8,128)(2,1)}, bf16[128,512]{1,0:T(8,128)(2,1)}, bf16[128,512]{1,0:T(8,128)(2,1)}) custom-call(bf16[1,32,2048]{2,1,0:T(8,128)(2,1)} %get-tuple-element.6.a, bf16[128,512]{1,0:T(8,128)(2,1)} %get-tuple-element.7.b, bf16[128,512]{1,0:T(8,128)(2,1)} %get-tuple-element.8.c), custom_call_target="tpu_custom_call" | custom-call | tf_op jit(solution)/shard_map/pallas_call | solution.py:289

commit v4 on v3

--- a/solution.py
+++ b/solution.py
@@ -19,7 +19,7 @@
 def kernel(
     recs, ctxs, q_ref, g_ref, k_ref, v_ref, surv_ref, counts_ref,
     dq_ref, dk_ref, dv_ref,
-    surv, live_counts, pos, qg, kv, acc, peer, dq_buf, dkv_buf,
+    surv, live_counts, pos, qg, kv, ds_buf, w_buf, acc, peer, dq_buf, dkv_buf,
     int_sem, pos_send, pos_recv, qg_send, qg_recv, kv_send, kv_recv, fwd_send,
     acc_send, acc_recv, dq_send, dq_recv, dkv_send, dkv_recv,
 ):
@@ -153,24 +153,30 @@
                     device_id=(r, zs * parts + part), device_id_type=MESH,
                 ).start()
 
-    for zs in reversed(range(groups)):
+    for zs in range(groups):
         blocks = (zs + 1) * parts
         length = blocks * tok
+        before = zs * parts * tok
         arrived(qg.at[zs], qg_recv.at[zs])
         q, g = qg[zs, 0], qg[zs, 1]
         keys = kv[0:blocks, 0].reshape(length, HEAD_DIM)
         vals = kv[0:blocks, 1].reshape(length, HEAD_DIM)
         scores = lax.dot_general(keys, q, NT, preferred_element_type=jnp.float32)
-        seen = lax.broadcasted_iota(jnp.int32, (length, slots), 0) <= place[zs : zs + 1, :]
-        scores = jnp.where(seen, scores * (factor * math.log2(math.e)), NEG_FILL)
+        scores = scores * (factor * math.log2(math.e))
+        position = place[zs : zs + 1, :]
+        seen = lax.broadcasted_iota(jnp.int32, (length - before, slots), 0) + before <= position
+        last = jnp.where(seen, scores[before:], NEG_FILL)
+        scores = jnp.concatenate([scores[:before], last], axis=0) if before else last
         top = jnp.maximum(jnp.max(scores, axis=0, keepdims=True), 0.1 * NEG_FILL)
         raw = jnp.exp2(scores - top)
         total = jnp.sum(raw, axis=0, keepdims=True)
-        weights = raw * (1.0 / jnp.maximum(total, 1e-30))
+        weights = raw * jnp.where(position >= 0, 1.0 / jnp.maximum(total, 1e-30), 0.0)
         grads = lax.dot_general(vals, g, NT, preferred_element_type=jnp.float32)
         delta = jnp.sum(weights * grads, axis=0, keepdims=True)
         ds = (weights * (grads - delta)).astype(jnp.bfloat16)
-        wb = weights.astype(jnp.bfloat16)
+        lanes = slice(zs * slots, (zs + 1) * slots)
+        ds_buf[0:length, lanes] = ds
+        w_buf[0:length, lanes] = weights.astype(jnp.bfloat16)
         dq = lax.dot_general(ds, keys, TN, preferred_element_type=jnp.float32)
         dq_buf[zs] = (dq * factor).astype(jnp.bfloat16)
         for rd in range(recs):
@@ -189,24 +195,21 @@
                     device_id=(rd, zs * parts + part), device_id_type=MESH,
                 ).start()
 
-        dk = lax.dot_general(ds, q, (((1,), (0,)), ((), ())), preferred_element_type=jnp.float32)
-        dv = lax.dot_general(wb, g, (((1,), (0,)), ((), ())), preferred_element_type=jnp.float32)
-        dk = dk.reshape(blocks, tok, HEAD_DIM)
-        dv = dv.reshape(blocks, tok, HEAD_DIM)
-        if zs == groups - 1:
-            acc[0:blocks, 0] = dk
-            acc[0:blocks, 1] = dv
-        else:
-            acc[0:blocks, 0] += dk
-            acc[0:blocks, 1] += dv
+    order = sorted(range(groups), key=lambda zs: (min(zs, groups - 1 - zs), -zs))
+    for step, zs in enumerate(order):
+        rows = slice(zs * parts * tok, (zs + 1) * parts * tok)
+        lanes = slice(zs * slots, groups * slots)
+        for i, buf in enumerate((ds_buf, w_buf)):
+            right = qg[zs:, i].reshape((groups - zs) * slots, HEAD_DIM)
+            term = jnp.dot(buf[rows, lanes], right, preferred_element_type=jnp.float32)
+            acc[zs * parts : (zs + 1) * parts, i] = term.reshape(parts, tok, HEAD_DIM)
         for dp in range(1, parts):
             cd = zs * parts + sibling(dp)
             send(acc.at[cd], peer.at[parts - dp, zs], acc_send.at[dp, zs],
                  acc_recv.at[parts - dp, zs], (r, z * parts + sibling(dp)))
-        if zs < groups - 1:
-            finish(zs + 1)
-    finish(0)
-
+        if step:
+            finish(order[step - 1])
+    finish(order[-1])
 
     for copy in sends:
         copy.wait_send()
@@ -265,6 +268,8 @@
             pltpu.VMEM((recs, 8, slots), jnp.int32),
             pltpu.VMEM((groups, 2, slots, HEAD_DIM), jnp.bfloat16),
             pltpu.VMEM((ctxs, 2, tok, HEAD_DIM), jnp.bfloat16),
+            pltpu.VMEM((ctxs * tok, groups * slots), jnp.bfloat16),
+            pltpu.VMEM((ctxs * tok, groups * slots), jnp.bfloat16),
             pltpu.VMEM((ctxs, 2, tok, HEAD_DIM), jnp.float32),
             pltpu.VMEM((parts, groups, 2, tok, HEAD_DIM), jnp.float32),
             pltpu.VMEM((groups, slots, HEAD_DIM), jnp.bfloat16),

time: 34.9 us -> 32.6 us (0.934)
  Pallas kernels: 34 us -> 31.8 us
    pallas_call x1, Pallas kernels: 32.3 us -> 30 us  [body(): pl.pallas_call(functools.partial(kernel, recs, ctxs), out_shape=(jax.Shap...]
where the time goes in v4:
time: 32.6 us; the launch traced here: 32.4 us
  Pallas kernels  31.8 us (98%)
  between operations  0.64 us (2%)
    pallas_call x1, Pallas kernels, body(): pl.pallas_call(functools.partial(kernel, recs, ctxs), out_shape=(jax.Shap...  30 us
    pallas_call x1, Pallas kernels, body(): pl.pallas_call(hand_over, out_shape=tuple((jax.ShapeDtypeStruct(a.shape,...  1.74 us

profile of v4, /device:TPU:0, one launch (start us, length us, event | category | flops | bytes accessed | tf_op | source)
XLA Modules:
  0.0 32.4 jit_solution(13763577217507465711)
XLA Ops:
  0.6 30.0 %shard_map.85 = (bf16[1,32,2048]{2,1,0:T(8,128)(2,1)}, bf16[128,512]{1,0:T(8,128)(2,1)}, bf16[128,512]{1,0:T(8,128)(2,1)}) custom-call(bf16[1,32,2048]{2,1,0:T(8,128)(2,1)} %q_ref.1, bf16[1,32,2048]{2,1,0:T(8,128)(2,1)} %g_ref.1, bf16[128,2048]{1,0:T(8,128)(2,1)} %k_ref.1, bf16[128,2048]{1,0:T(8,128)(2,1)} %v_ref.1, s32[1,256]{1,0:T(1,128)} %surv_ref.1, ...), custom_call_target="tpu_custom_call" | custom-call | flops 671088640 | bytes 1048576 | tf_op jit(solution)/shard_map/pallas_call | solution.py:256
  30.7 1.7 %shard_map.86 = (bf16[1,32,2048]{2,1,0:T(8,128)(2,1)}, bf16[128,512]{1,0:T(8,128)(2,1)}, bf16[128,512]{1,0:T(8,128)(2,1)}) custom-call(bf16[1,32,2048]{2,1,0:T(8,128)(2,1)} %get-tuple-element.6.a, bf16[128,512]{1,0:T(8,128)(2,1)} %get-tuple-element.7.b, bf16[128,512]{1,0:T(8,128)(2,1)} %get-tuple-element.8.c), custom_call_target="tpu_custom_call" | custom-call | tf_op jit(solution)/shard_map/pallas_call | solution.py:294

commit v5 on v4

--- a/solution.py
+++ b/solution.py
@@ -39,8 +39,16 @@
 
     others = [(dr, dz) for dz in range(groups) for dr in range(recs) if dr or dz]
 
+    def flip(index, bits):
+        bit = 1
+        while bit <= bits:
+            if bits & bit:
+                index = index + bit * (1 - 2 * (index // bit % 2))
+            bit *= 2
+        return index
+
     def partner(dr, dz):
-        return (lax.rem(r + dr, recs), lax.rem(z + dz, groups))
+        return (flip(r, dr), flip(z, dz))
 
     def sibling(dp):
         return lax.rem(part + dp, parts)
@@ -94,18 +102,30 @@
         copy.start()
         sends.append(copy)
 
-    for dz in range(1, groups):
-        pz = lax.rem(z + dz, groups)
+    def send_keys(dz):
+        pz = flip(z, dz)
         for i, ref in enumerate((k_ref, v_ref)):
             send(ref.at[:, head_cols(r, pz)], kv.at[c, i], kv_send.at[dz, i], kv_recv.at[c],
                  (r, pz * parts + part))
+
+    def send_queries(dz):
+        for dr in range(recs):
+            if dr or dz:
+                pr, pz = partner(dr, dz)
+                for i, ref in enumerate((q_ref, g_ref)):
+                    send(ref.at[0, :, head_cols(pr, pz)], qg.at[z, i, rows_r, :],
+                         qg_send.at[dz, dr, i], qg_recv.at[z], (pr, pz * parts + part))
+
+    far = [dz for dz in reversed(range(1, groups)) if 2 * dz >= groups]
+    near = [dz for dz in reversed(range(1, groups)) if 2 * dz < groups]
+    for some in (far, near):
+        for dz in some:
+            send_keys(dz)
+        for dz in some:
+            send_queries(dz)
+    send_queries(0)
     for dr in range(1, recs):
-        send(pos.at[r], pos.at[r], pos_send.at[dr], pos_recv.at[r], (lax.rem(r + dr, recs), c))
-    for dr, dz in others:
-        pr, pz = partner(dr, dz)
-        for i, ref in enumerate((q_ref, g_ref)):
-            send(ref.at[0, :, head_cols(pr, pz)], qg.at[z, i, rows_r, :],
-                 qg_send.at[dz, dr, i], qg_recv.at[z], (pr, pz * parts + part))
+        send(pos.at[r], pos.at[r], pos_send.at[dr], pos_recv.at[r], (flip(r, dr), c))
     for dp in range(1, parts):
         for i, ref in enumerate((k_ref, v_ref)):
             send(ref.at[:, head_cols(r, z)], kv.at[c, i], fwd_send.at[dp, 0, i], kv_recv.at[c],
@@ -114,20 +134,16 @@
     def arrived(ref, sem):
         pltpu.make_async_copy(ref, ref, sem).wait()
 
-    for dz in range(1, groups):
-        cs = lax.rem(z + dz, groups) * parts + part
+    for dz in far + near:
+        cs = flip(z, dz) * parts + part
         arrived(kv.at[cs], kv_recv.at[cs])
         for dp in range(1, parts):
             send(kv.at[cs], kv.at[cs], fwd_send.at[dp, dz, 0], kv_recv.at[cs],
                  (r, z * parts + sibling(dp)))
     arrived(kv.at[c], kv_recv.at[c])
     for dr in range(1, recs):
-        rs = lax.rem(r + dr, recs)
+        rs = flip(r, dr)
         arrived(pos.at[rs], pos_recv.at[rs])
-    for dz in range(groups):
-        for dp in range(1, parts):
-            cs = lax.rem(z + dz, groups) * parts + sibling(dp)
-            arrived(kv.at[cs], kv_recv.at[cs])
 
     place = sum(pos[rs] for rs in range(recs)) - 1
 
@@ -157,6 +173,9 @@
         blocks = (zs + 1) * parts
         length = blocks * tok
         before = zs * parts * tok
+        for dp in range(1, parts):
+            cs = zs * parts + sibling(dp)
+            arrived(kv.at[cs], kv_recv.at[cs])
         arrived(qg.at[zs], qg_recv.at[zs])
         q, g = qg[zs, 0], qg[zs, 1]
         keys = kv[0:blocks, 0].reshape(length, HEAD_DIM)

time: 32.6 us -> 32.4 us (level)
  no operation moved by 1% of the time
where the time goes in v5:
time: 32.4 us; the launch traced here: 32.2 us
  Pallas kernels  31.5 us (97%)
  between operations  0.64 us (2%)
    pallas_call x1, Pallas kernels, body(): pl.pallas_call(functools.partial(kernel, recs, ctxs), out_shape=(jax.Shap...  29.8 us
    pallas_call x1, Pallas kernels, body(): pl.pallas_call(hand_over, out_shape=tuple((jax.ShapeDtypeStruct(a.shape,...  1.74 us

profile of v5, /device:TPU:0, one launch (start us, length us, event | category | flops | bytes accessed | tf_op | source)
XLA Modules:
  0.0 32.2 jit_solution(14011063831028115255)
XLA Ops:
  0.6 29.8 %shard_map.85 = (bf16[1,32,2048]{2,1,0:T(8,128)(2,1)}, bf16[128,512]{1,0:T(8,128)(2,1)}, bf16[128,512]{1,0:T(8,128)(2,1)}) custom-call(bf16[1,32,2048]{2,1,0:T(8,128)(2,1)} %q_ref.1, bf16[1,32,2048]{2,1,0:T(8,128)(2,1)} %g_ref.1, bf16[128,2048]{1,0:T(8,128)(2,1)} %k_ref.1, bf16[128,2048]{1,0:T(8,128)(2,1)} %v_ref.1, s32[1,256]{1,0:T(1,128)} %surv_ref.1, ...), custom_call_target="tpu_custom_call" | custom-call | flops 671088640 | bytes 1048576 | tf_op jit(solution)/shard_map/pallas_call | solution.py:275
  30.4 1.7 %shard_map.86 = (bf16[1,32,2048]{2,1,0:T(8,128)(2,1)}, bf16[128,512]{1,0:T(8,128)(2,1)}, bf16[128,512]{1,0:T(8,128)(2,1)}) custom-call(bf16[1,32,2048]{2,1,0:T(8,128)(2,1)} %get-tuple-element.6.a, bf16[128,512]{1,0:T(8,128)(2,1)} %get-tuple-element.7.b, bf16[128,512]{1,0:T(8,128)(2,1)} %get-tuple-element.8.c), custom_call_target="tpu_custom_call" | custom-call | tf_op jit(solution)/shard_map/pallas_call | solution.py:313

commit v6 on v4

--- a/solution.py
+++ b/solution.py
@@ -37,10 +37,14 @@
     def head_cols(rec, group):
         return pl.ds(pl.multiple_of((rec * groups + group) * HEAD_DIM, HEAD_DIM), HEAD_DIM)
 
-    others = [(dr, dz) for dz in range(groups) for dr in range(recs) if dr or dz]
-
-    def partner(dr, dz):
-        return (lax.rem(r + dr, recs), lax.rem(z + dz, groups))
+    def loop(low, high, step):
+        lax.fori_loop(low, high, lambda i, carry: (step(i), carry)[1], 0)
+
+    def turn_rec(dr):
+        return lax.rem(r + dr, recs)
+
+    def turn_group(dz):
+        return lax.rem(z + dz, groups)
 
     def sibling(dp):
         return lax.rem(part + dp, parts)
@@ -53,9 +57,14 @@
         copy.start()
 
     barrier = pltpu.get_barrier_semaphore()
-    for dr, dz in others:
-        pr, pz = partner(dr, dz)
-        pl.semaphore_signal(barrier, inc=1, device_id=(pr, pz * parts + part), device_id_type=MESH)
+    def greet(i):
+        pl.semaphore_signal(
+            barrier, inc=1,
+            device_id=(turn_rec(lax.rem(i, recs)), turn_group(i // recs) * parts + part),
+            device_id_type=MESH,
+        )
+
+    loop(1, recs * groups, greet)
     for dp in range(1, parts):
         pl.semaphore_signal(
             barrier, inc=1, device_id=(r, z * parts + sibling(dp)), device_id_type=MESH
@@ -82,52 +91,75 @@
         live = (here >= 0) & (here < cap) & (here < live_counts[0, cs])
         pos[r, zs : zs + 1, :] = jnp.where(live, moved[0:1, 0:slots] + cs * tok + 1, 0)
 
-    pl.semaphore_wait(barrier, len(others) + parts - 1)
-
-    sends = []
-
-    def send(src, dst, send_sem, recv_sem, device):
-        copy = pltpu.make_async_remote_copy(
+    pl.semaphore_wait(barrier, recs * groups + parts - 2)
+
+    def remote(src, dst, send_sem, recv_sem, device):
+        return pltpu.make_async_remote_copy(
             src_ref=src, dst_ref=dst, send_sem=send_sem, recv_sem=recv_sem,
             device_id=device, device_id_type=MESH,
         )
-        copy.start()
-        sends.append(copy)
-
-    for dz in range(1, groups):
-        pz = lax.rem(z + dz, groups)
-        for i, ref in enumerate((k_ref, v_ref)):
-            send(ref.at[:, head_cols(r, pz)], kv.at[c, i], kv_send.at[dz, i], kv_recv.at[c],
-                 (r, pz * parts + part))
-    for dr in range(1, recs):
-        send(pos.at[r], pos.at[r], pos_send.at[dr], pos_recv.at[r], (lax.rem(r + dr, recs), c))
-    for dr, dz in others:
-        pr, pz = partner(dr, dz)
-        for i, ref in enumerate((q_ref, g_ref)):
-            send(ref.at[0, :, head_cols(pr, pz)], qg.at[z, i, rows_r, :],
-                 qg_send.at[dz, dr, i], qg_recv.at[z], (pr, pz * parts + part))
-    for dp in range(1, parts):
-        for i, ref in enumerate((k_ref, v_ref)):
-            send(ref.at[:, head_cols(r, z)], kv.at[c, i], fwd_send.at[dp, 0, i], kv_recv.at[c],
-                 (r, z * parts + sibling(dp)))
 
     def arrived(ref, sem):
         pltpu.make_async_copy(ref, ref, sem).wait()
 
-    for dz in range(1, groups):
-        cs = lax.rem(z + dz, groups) * parts + part
+    def key_copies(dz):
+        pz = turn_group(dz)
+        return [
+            remote(ref.at[:, head_cols(r, pz)], kv.at[c, i], kv_send.at[dz, i], kv_recv.at[c],
+                   (r, pz * parts + part))
+            for i, ref in enumerate((k_ref, v_ref))
+        ]
+
+    def query_copies(n):
+        dr, dz = lax.rem(n, recs), n // recs
+        pr, pz = turn_rec(dr), turn_group(dz)
+        return [
+            remote(ref.at[0, :, head_cols(pr, pz)], qg.at[z, i, rows_r, :],
+                   qg_send.at[dz, dr, i], qg_recv.at[z], (pr, pz * parts + part))
+            for i, ref in enumerate((q_ref, g_ref))
+        ]
+
+    def own_key_copies(dp):
+        return [
+            remote(ref.at[:, head_cols(r, z)], kv.at[c, i], fwd_send.at[dp, 0, i], kv_recv.at[c],
+                   (r, z * parts + sibling(dp)))
+            for i, ref in enumerate((k_ref, v_ref))
+        ]
+
+    def handed_on(dz, dp):
+        cs = turn_group(dz) * parts + part
+        return remote(kv.at[cs], kv.at[cs], fwd_send.at[dp, dz, 0], kv_recv.at[cs],
+                      (r, z * parts + sibling(dp)))
+
+    def place_copy(dr):
+        return remote(pos.at[r], pos.at[r], pos_send.at[dr], pos_recv.at[r], (turn_rec(dr), c))
+
+    def sums_copy(zs, dp):
+        return remote(acc.at[zs * parts + sibling(dp)], peer.at[parts - dp, zs],
+                      acc_send.at[dp, zs], acc_recv.at[parts - dp, zs],
+                      (r, z * parts + sibling(dp)))
+
+    def start(copies):
+        for copy in copies:
+            copy.start()
+
+    def wait_sent(copies):
+        for copy in copies:
+            copy.wait_send()
+
+    loop(1, groups, lambda dz: start(key_copies(dz)))
+    loop(1, recs, lambda dr: start([place_copy(dr)]))
+    loop(1, recs * groups, lambda n: start(query_copies(n)))
+    loop(1, parts, lambda dp: start(own_key_copies(dp)))
+
+    def hand_on(dz):
+        cs = turn_group(dz) * parts + part
         arrived(kv.at[cs], kv_recv.at[cs])
-        for dp in range(1, parts):
-            send(kv.at[cs], kv.at[cs], fwd_send.at[dp, dz, 0], kv_recv.at[cs],
-                 (r, z * parts + sibling(dp)))
+        loop(1, parts, lambda dp: start([handed_on(dz, dp)]))
+
+    loop(1, groups, hand_on)
     arrived(kv.at[c], kv_recv.at[c])
-    for dr in range(1, recs):
-        rs = lax.rem(r + dr, recs)
-        arrived(pos.at[rs], pos_recv.at[rs])
-    for dz in range(groups):
-        for dp in range(1, parts):
-            cs = lax.rem(z + dz, groups) * parts + sibling(dp)
-            arrived(kv.at[cs], kv_recv.at[cs])
+    loop(1, recs, lambda dr: arrived(pos.at[turn_rec(dr)], pos_recv.at[turn_rec(dr)]))
 
     place = sum(pos[rs] for rs in range(recs)) - 1
 
@@ -157,6 +189,9 @@
         blocks = (zs + 1) * parts
         length = blocks * tok
         before = zs * parts * tok
+        for dp in range(1, parts):
+            cs = zs * parts + sibling(dp)
+            arrived(kv.at[cs], kv_recv.at[cs])
         arrived(qg.at[zs], qg_recv.at[zs])
         q, g = qg[zs, 0], qg[zs, 1]
         keys = kv[0:blocks, 0].reshape(length, HEAD_DIM)
@@ -179,8 +214,9 @@
         w_buf[0:length, lanes] = weights.astype(jnp.bfloat16)
         dq = lax.dot_general(ds, keys, TN, preferred_element_type=jnp.float32)
         dq_buf[zs] = (dq * factor).astype(jnp.bfloat16)
-        for rd in range(recs):
-            src = dq_buf.at[zs, rd * cap : (rd + 1) * cap, :]
+
+        def send_home(rd):
+            src = dq_buf.at[zs, pl.ds(pl.multiple_of(rd * cap, cap), cap), :]
             dst = dq_ref.at[0, :, head_cols(r, z)]
             home = (r == rd) & (z == zs)
 
@@ -190,10 +226,9 @@
 
             @pl.when(jnp.logical_not(home))
             def _():
-                pltpu.make_async_remote_copy(
-                    src_ref=src, dst_ref=dst, send_sem=dq_send.at[zs, rd], recv_sem=dq_recv,
-                    device_id=(rd, zs * parts + part), device_id_type=MESH,
-                ).start()
+                remote(src, dst, dq_send.at[zs, rd], dq_recv, (rd, zs * parts + part)).start()
+
+        loop(0, recs, send_home)
 
     order = sorted(range(groups), key=lambda zs: (min(zs, groups - 1 - zs), -zs))
     for step, zs in enumerate(order):
@@ -203,29 +238,33 @@
             right = qg[zs:, i].reshape((groups - zs) * slots, HEAD_DIM)
             term = jnp.dot(buf[rows, lanes], right, preferred_element_type=jnp.float32)
             acc[zs * parts : (zs + 1) * parts, i] = term.reshape(parts, tok, HEAD_DIM)
-        for dp in range(1, parts):
-            cd = zs * parts + sibling(dp)
-            send(acc.at[cd], peer.at[parts - dp, zs], acc_send.at[dp, zs],
-                 acc_recv.at[parts - dp, zs], (r, z * parts + sibling(dp)))
+        loop(1, parts, lambda dp: start([sums_copy(zs, dp)]))
         if step:
             finish(order[step - 1])
     finish(order[-1])
 
-    for copy in sends:
-        copy.wait_send()
-    for zs in range(groups):
-        for rd in range(recs):
-
-            @pl.when(jnp.logical_not((r == rd) & (z == zs)))
-            def _():
-                arrived(dq_buf.at[zs, rd * cap : (rd + 1) * cap, :], dq_send.at[zs, rd])
-
-        for i in range(2):
-
-            @pl.when(z != zs)
-            def _():
+    loop(1, groups, lambda dz: wait_sent(key_copies(dz)))
+    loop(1, recs, lambda dr: wait_sent([place_copy(dr)]))
+    loop(1, recs * groups, lambda n: wait_sent(query_copies(n)))
+    loop(1, parts, lambda dp: wait_sent(own_key_copies(dp)))
+    loop(1, groups, lambda dz: loop(1, parts, lambda dp: wait_sent([handed_on(dz, dp)])))
+    loop(0, groups, lambda zs: loop(1, parts, lambda dp: wait_sent([sums_copy(zs, dp)])))
+
+    def sent_home(n):
+        zs, rd = n // recs, lax.rem(n, recs)
+
+        @pl.when(jnp.logical_not((r == rd) & (z == zs)))
+        def _():
+            arrived(dq_buf.at[zs, pl.ds(pl.multiple_of(rd * cap, cap), cap), :], dq_send.at[zs, rd])
+
+    def sums_sent(zs):
+        @pl.when(z != zs)
+        def _():
+            for i in range(2):
                 arrived(dkv_buf.at[zs, i], dkv_send.at[zs, i])
 
+    loop(0, recs * groups, sent_home)
+    loop(0, groups, sums_sent)
     arrived(dq_ref, dq_recv)
     arrived(dk_ref, dkv_recv.at[0])
     arrived(dv_ref, dkv_recv.at[1])

time: 32.6 us -> 32.6 us (level)
  no operation moved by 1% of the time
where the time goes in v6:
time: 32.6 us; the launch traced here: 32.4 us
  Pallas kernels  31.8 us (98%)
  between operations  0.64 us (2%)
    pallas_call x1, Pallas kernels, body(): pl.pallas_call(functools.partial(kernel, recs, ctxs), out_shape=(jax.Shap...  30.1 us
    pallas_call x1, Pallas kernels, body(): pl.pallas_call(hand_over, out_shape=tuple((jax.ShapeDtypeStruct(a.shape,...  1.74 us

profile of v6, /device:TPU:0, one launch (start us, length us, event | category | flops | bytes accessed | tf_op | source)
XLA Modules:
  0.0 32.4 jit_solution(13714541376791571662)
XLA Ops:
  0.6 30.1 %shard_map.85 = (bf16[1,32,2048]{2,1,0:T(8,128)(2,1)}, bf16[128,512]{1,0:T(8,128)(2,1)}, bf16[128,512]{1,0:T(8,128)(2,1)}) custom-call(bf16[1,32,2048]{2,1,0:T(8,128)(2,1)} %q_ref.1, bf16[1,32,2048]{2,1,0:T(8,128)(2,1)} %g_ref.1, bf16[128,2048]{1,0:T(8,128)(2,1)} %k_ref.1, bf16[128,2048]{1,0:T(8,128)(2,1)} %v_ref.1, s32[1,256]{1,0:T(1,128)} %surv_ref.1, ...), custom_call_target="tpu_custom_call" | custom-call | flops 671088640 | bytes 1048576 | tf_op jit(solution)/shard_map/pallas_call | solution.py:295
  30.7 1.7 %shard_map.86 = (bf16[1,32,2048]{2,1,0:T(8,128)(2,1)}, bf16[128,512]{1,0:T(8,128)(2,1)}, bf16[128,512]{1,0:T(8,128)(2,1)}) custom-call(bf16[1,32,2048]{2,1,0:T(8,128)(2,1)} %get-tuple-element.6.a, bf16[128,512]{1,0:T(8,128)(2,1)} %get-tuple-element.7.b, bf16[128,512]{1,0:T(8,128)(2,1)} %get-tuple-element.8.c), custom_call_target="tpu_custom_call" | custom-call | tf_op jit(solution)/shard_map/pallas_call | solution.py:333
